TPU v7x, 32 devices: a whole 2x2x4 slice. The times are simulated.
32 devices in a mesh: row: 8 (over z, y), col: 4 (over x, core).
Axes of the slice: x: 2, y: 2, z: 4, core: 2. Of those that a mesh axis runs over, the one named last changes fastest.
Arguments:
- start_values: float32 [44, 4, 2, 256], P(None, 'col', None, 'row'), may hold values from -6 to 6
- cosine: float32 [256], P('row'), may hold values from -0.99 to 0.99
- arc_index: int32 [256], P('row'), may hold values from 0 to 7, never falling along the last dimension, each value on 1 to 128 neighbouring positions
- arc_weight: float32 [8], replicated, may hold values from 0.003 to 0.03
- observed: float32 [256], P('row'), may hold values from -12 to 12
- orientation_term: float32 [256, 44, 4, 128], P('row', None, 'col'), may hold values from -3 to 3
- step_gain: float32 [44, 4, 128], replicated, may hold values from 1.5 to 1.9
- step_damp: float32 [44, 4, 128], replicated, may hold values from 0.94 to 1
Outputs:
- normal_update: float32 [4, 1024, 44, 512], P(None, 'row', None, 'col')
- rhs_update: float32 [44, 4, 128], P(None, 'col')
Inputs may be any that keep to these rules, and one draw needn't show every extreme that they name: `arc_index`: Non-decreasing along the observations; each arc names 1 to 128 consecutive observations.
All inputs are finite; a program needn't handle non-finite values.
Results may differ from a plain program's by a relative error of at most 0.000073.
Values sent between devices are 32-bit elements; how exact they have to be, the bound alone decides.
A program may use at most 128 MiB of HBM per device.

v0:
```python
import functools
import jax
import jax.numpy as jnp
from jax import lax
from jax.experimental import pallas as pl
from jax.experimental.pallas import tpu as pltpu
from jax.sharding import PartitionSpec as P

RT = 4
LANES = 128
MESH = pl.DeviceIdType.MESH


def gather_kernel(
    sizes,
    arc_weight, start, cosine, arc_index, observed, gain, damp, orient,
    split_out, lhs_hi, lhs_lo, rhs_out,
    every, split, forcing, f_t, g_t, d_t, q_t, slab, wsend, wblocks, wcol, ocol,
    fsem, osem, rsem, xsem, wrsem, slsem, up_sem, down_sem, y_sem, x_send, w_send, sl_send,
):
    rows, cols, tiles, obs = sizes
    line = rows // 2
    per = LANES // obs
    half = per // 2
    chunks = tiles // per
    r = lax.axis_index("row")
    c = lax.axis_index("col")
    u = r // 2
    v = r % 2
    even = u % 2 == 0
    mate = u + 1 - 2 * (u % 2)
    owner = r % cols
    stride = rows // cols
    slab_chunk = ((RT - 1) * stride + stride - 1) // per

    def row_of(uu, vv):
        return uu * 2 + vv

    barrier = pltpu.get_barrier_semaphore()
    for d in range(1, rows):
        pl.semaphore_signal(barrier, inc=1, device_id=((r + d) % rows, c), device_id_type=MESH)
    for d in range(1, cols):
        pl.semaphore_signal(barrier, inc=1, device_id=(r, (c + d) % cols), device_id_type=MESH)

    def fetch(j):
        return pltpu.make_async_copy(orient.at[:, j, 0, :], forcing.at[j], fsem.at[j])

    @pl.loop(0, tiles)
    def _(j):
        fetch(j).start()

    index = arc_index[...]
    weight = jnp.zeros(index.shape, jnp.float32)
    for k in range(arc_weight.shape[0]):
        weight = weight + jnp.where(index == k, arc_weight[k], 0.0)
    wsend[...] = jnp.zeros_like(wsend)
    wsend[0:1, 0:obs] = weight
    wsend[1:2, 0:obs] = weight * observed[...]
    cos_row = jnp.concatenate([cosine[...]] * per, axis=1)

    def block(t, src, low=0, count=per):
        return every.at[pl.ds(t * per + low, count), pl.ds(pl.multiple_of(src * obs, obs), obs), :]

    def send(t, src, to_row, send_sem, recv_sem, low=0, count=per):
        pltpu.make_async_remote_copy(
            src_ref=block(t, src, low, count),
            dst_ref=block(t, src, low, count),
            send_sem=send_sem,
            recv_sem=recv_sem,
            device_id=(to_row, c),
            device_id_type=MESH,
        ).start()

    def arrived(t, src, sem, low=0, count=per):
        ref = block(t, src, low, count)
        pltpu.make_async_copy(ref, ref, sem).wait()

    def slab_tile(i):
        return i * stride + r // cols

    def relay(t, src):
        @pl.when((t == slab_chunk) & (c == owner))
        def _():
            spot = pl.ds(pl.multiple_of(src * obs, obs), obs)

            @pl.loop(0, RT)
            def _(i):
                for d in range(1, cols):
                    pltpu.make_async_remote_copy(
                        src_ref=every.at[slab_tile(i), spot, :],
                        dst_ref=slab.at[i, spot, :],
                        send_sem=sl_send.at[d],
                        recv_sem=slsem.at[i, src],
                        device_id=(r, (c + d) % cols),
                        device_id_type=MESH,
                    ).start()

    def columns(ref, t):
        parts = [jnp.broadcast_to(ref[t * per + q, pl.ds(c, 1), :], (obs, LANES)) for q in range(per)]
        return jnp.concatenate(parts, axis=0).T

    def recurrence(t):
        for q in range(per):
            fetch(t * per + q).wait()
        f_t[...] = forcing[pl.ds(t * per, per)].reshape(LANES, LANES).T
        g_t[...] = columns(gain, t) * cos_row
        d_t[...] = columns(damp, t)
        first = jnp.concatenate([start[t * per + q, 0, 0:1, :] for q in range(per)], axis=1)
        second = jnp.concatenate([start[t * per + q, 0, 1:2, :] for q in range(per)], axis=1)

        def step(m, state):
            prev_two, prev_one = state
            for k in range(8):
                at = pl.ds(m * 8 + k, 1)
                current = g_t[at, :] * prev_one + (f_t[at, :] - d_t[at, :] * prev_two)
                q_t[at, :] = current
                prev_two, prev_one = prev_one, current
            return prev_two, prev_one

        lax.fori_loop(0, LANES // 8, step, (first, second))
        own = pl.ds(pl.multiple_of(r * obs, obs), obs)
        every[pl.ds(t * per, per), own, :] = q_t[...].T.reshape(per, obs, LANES)

    def own_sends(t):
        @pl.when(u < line - 1)
        def _():
            send(t, r, row_of(u + 1, v), up_sem.at[0], rsem.at[r, t])

        @pl.when(u > 0)
        def _():
            send(t, r, row_of(u - 1, v), down_sem.at[0], rsem.at[r, t])

        send(t, r, row_of(u, 1 - v), y_sem.at[0], rsem.at[r, t])
        relay(t, r)

    recurrence(0)
    pl.semaphore_wait(barrier, rows - 1 + cols - 1)
    for d in range(1, rows):
        pltpu.make_async_remote_copy(
            src_ref=wsend,
            dst_ref=wblocks.at[r],
            send_sem=w_send.at[d],
            recv_sem=wrsem.at[r],
            device_id=((r + d) % rows, c),
            device_id_type=MESH,
        ).start()
    wblocks[r] = wsend[...]
    own_sends(0)

    @pl.loop(1, chunks)
    def _(t):
        recurrence(t)
        own_sends(t)

    for p in range(1, line):
        @pl.loop(0, chunks)
        def _(t, p=p):
            @pl.when(u >= p)
            def _():
                src = row_of(u - p, v)
                arrived(t, src, rsem.at[src, t])

                @pl.when(u < line - 1)
                def _():
                    send(t, src, row_of(u + 1, v), up_sem.at[p], rsem.at[src, t])

                def whole():
                    send(t, src, row_of(u, 1 - v), y_sem.at[p], rsem.at[src, t])

                if p == 1:
                    pl.when(even)(whole)

                    @pl.when(jnp.logical_not(even))
                    def _():
                        send(t, src, row_of(u, 1 - v), y_sem.at[p], rsem.at[src, t], half, per - half)
                else:
                    whole()
                relay(t, src)

            @pl.when(u + p < line)
            def _():
                src = row_of(u + p, v)
                arrived(t, src, rsem.at[src, t])

                @pl.when(u > 0)
                def _():
                    send(t, src, row_of(u - 1, v), down_sem.at[p], rsem.at[src, t])

                def whole():
                    send(t, src, row_of(u, 1 - v), y_sem.at[line + p], rsem.at[src, t])

                if p == 1:
                    pl.when(jnp.logical_not(even))(whole)

                    @pl.when(even)
                    def _():
                        send(t, src, row_of(u, 1 - v), y_sem.at[line + p], rsem.at[src, t], half, per - half)
                else:
                    whole()
                relay(t, src)

    across = row_of(u, 1 - v)

    @pl.loop(0, chunks)
    def _(t):
        arrived(t, across, rsem.at[across, t])
        send(t, across, row_of(mate, v), x_send, xsem.at[t], 0, half)
        relay(t, across)

    for d in range(1, rows):
        src = (r + d) % rows
        pltpu.make_async_copy(wblocks.at[src], wblocks.at[src], wrsem.at[src]).wait()

    @pl.loop(0, rows)
    def _(src):
        turned = wblocks[src].T
        spot = pl.ds(pl.multiple_of(src * obs, obs), obs)
        wcol[spot, :] = jnp.broadcast_to(turned[0:obs, 0:1], (obs, LANES))
        ocol[spot, :] = jnp.broadcast_to(turned[0:obs, 1:2], (obs, LANES))

    total = rows * obs

    def put(t):
        spot = pl.ds(t * per, per)
        return pltpu.make_async_copy(split.at[spot], split_out.at[spot], osem.at[t])

    @pl.loop(0, chunks)
    def _(t):
        for p in range(1, line):
            for sign in (-1, 1):
                far = u + sign * p

                @pl.when((far >= 0) & (far < line))
                def _(p=p, far=far):
                    src = row_of(far, 1 - v)
                    if p == 1:
                        @pl.when(far == mate)
                        def _():
                            arrived(t, src, rsem.at[src, t], half, per - half)
                            arrived(t, src, xsem.at[t], 0, half)

                        @pl.when(far != mate)
                        def _():
                            arrived(t, src, rsem.at[src, t])
                    else:
                        arrived(t, src, rsem.at[src, t])
                    relay(t, src)

        @pl.loop(0, per)
        def _(q):
            j = t * per + q
            values = every[j]
            rhs_out[pl.ds(j, 1), :] = jnp.sum(values * ocol[...], axis=0, keepdims=True)
            high = values.astype(jnp.bfloat16)
            split[j, 0:total, :] = high
            split[j, total:2 * total, :] = (values - high.astype(jnp.float32)).astype(jnp.bfloat16)

        put(t).start()

    @pl.when(c == owner)
    def _():
        @pl.loop(0, RT)
        def _(i):
            slab[i] = every[slab_tile(i)]

    @pl.when(c != owner)
    def _():
        @pl.loop(0, rows)
        def _(src):
            @pl.loop(0, RT)
            def _(i):
                ref = slab.at[i, pl.ds(pl.multiple_of(src * obs, obs), obs), :]
                pltpu.make_async_copy(ref, ref, slsem.at[i, src]).wait()

    for i in range(RT):
        turned = (slab[i] * wcol[...]).T
        high = turned.astype(jnp.bfloat16)
        at = slice(i * LANES, (i + 1) * LANES)
        lhs_hi[at, 0:total] = high
        lhs_hi[at, total:2 * total] = high
        lhs_lo[at, :] = (turned - high.astype(jnp.float32)).astype(jnp.bfloat16)

    def left(sem, low=0, count=tiles):
        ref = every.at[pl.ds(low, count), pl.ds(0, obs), :]
        pltpu.make_async_copy(ref, ref, sem).wait()

    for p in range(line):
        pl.when((u >= p) & (u < line - 1))(functools.partial(left, up_sem.at[p]))
        pl.when((u + p < line) & (u > 0))(functools.partial(left, down_sem.at[p]))
    left(y_sem.at[0])
    part = chunks * (per - half)
    for p in range(1, line):
        if p == 1:
            pl.when((u >= p) & even)(functools.partial(left, y_sem.at[p]))
            pl.when((u >= p) & jnp.logical_not(even))(functools.partial(left, y_sem.at[p], 0, part))
            pl.when((u + p < line) & jnp.logical_not(even))(functools.partial(left, y_sem.at[line + p]))
            pl.when((u + p < line) & even)(functools.partial(left, y_sem.at[line + p], 0, part))
        else:
            pl.when(u >= p)(functools.partial(left, y_sem.at[p]))
            pl.when(u + p < line)(functools.partial(left, y_sem.at[line + p]))
    left(x_send, 0, chunks * half)
    for d in range(1, rows):
        pltpu.make_async_copy(wsend, wsend, w_send.at[d]).wait()

    @pl.when(c == owner)
    def _():
        for d in range(1, cols):
            pltpu.make_async_copy(slab, slab, sl_send.at[d]).wait()

    @pl.loop(0, chunks)
    def _(t):
        put(t).wait()


def gather(sizes, *operands):
    rows, cols, tiles, obs = sizes
    total = rows * obs
    per = LANES // obs
    chunks = tiles // per
    line = rows // 2
    vmem = pl.BlockSpec(memory_space=pltpu.VMEM)
    anywhere = pl.BlockSpec(memory_space=pl.ANY)
    smem = pl.BlockSpec(memory_space=pltpu.SMEM)
    dma = pltpu.SemaphoreType.DMA
    square = pltpu.VMEM((LANES, LANES), jnp.float32)
    return pl.pallas_call(
        functools.partial(gather_kernel, sizes),
        out_shape=(
            jax.ShapeDtypeStruct((tiles, 2 * total, LANES), jnp.bfloat16),
            jax.ShapeDtypeStruct((RT * LANES, 2 * total), jnp.bfloat16),
            jax.ShapeDtypeStruct((RT * LANES, total), jnp.bfloat16),
            jax.ShapeDtypeStruct((tiles, LANES), jnp.float32),
        ),
        in_specs=[smem] + [vmem] * 6 + [anywhere],
        out_specs=(anywhere, vmem, vmem, vmem),
        scratch_shapes=[
            pltpu.VMEM((tiles, total, LANES), jnp.float32),
            pltpu.VMEM((tiles, 2 * total, LANES), jnp.bfloat16),
            pltpu.VMEM((tiles, obs, LANES), jnp.float32),
            square, square, square, square,
            pltpu.VMEM((RT, total, LANES), jnp.float32),
            pltpu.VMEM((8, LANES), jnp.float32),
            pltpu.VMEM((rows, 8, LANES), jnp.float32),
            pltpu.VMEM((total, LANES), jnp.float32),
            pltpu.VMEM((total, LANES), jnp.float32),
            dma((tiles,)), dma((chunks,)), dma((rows, chunks)), dma((chunks,)), dma((rows,)),
            dma((RT, rows)), dma((line,)), dma((line,)), dma((2 * line,)), dma(()), dma((rows,)),
            dma((cols,)),
        ],
        compiler_params=pltpu.CompilerParams(
            collective_id=0, has_side_effects=True, vmem_limit_bytes=56 << 20
        ),
        name="gather_design",
    )(*operands)


def multiply_kernel(total, lhs_hi, lhs_lo, split, out):
    count = split.shape[0]
    for j in range(0, count, 2):
        pair = jnp.concatenate([split[j], split[j + 1]], axis=1)
        product = jnp.dot(lhs_hi[...], pair, preferred_element_type=jnp.float32)
        product += jnp.dot(lhs_lo[...], pair[0:total], preferred_element_type=jnp.float32)
        for k in range(2):
            piece = product[:, k * LANES:(k + 1) * LANES]
            out[:, :, j + k, :] = piece.reshape(RT, LANES, LANES)


def multiply(sizes, lhs_hi, lhs_lo, split):
    rows, cols, tiles, obs = sizes
    total = rows * obs
    group = 8
    return pl.pallas_call(
        functools.partial(multiply_kernel, total),
        grid=(pl.cdiv(tiles, group),),
        out_shape=jax.ShapeDtypeStruct((RT, LANES, tiles, LANES), jnp.float32),
        in_specs=[
            pl.BlockSpec(lhs_hi.shape, lambda g: (0, 0)),
            pl.BlockSpec(lhs_lo.shape, lambda g: (0, 0)),
            pl.BlockSpec((group, 2 * total, LANES), lambda g: (g, 0, 0)),
        ],
        out_specs=pl.BlockSpec((RT, LANES, group, LANES), lambda g: (0, 0, g, 0)),
        compiler_params=pltpu.CompilerParams(vmem_limit_bytes=48 << 20),
        name="slab_product",
    )(lhs_hi, lhs_lo, split)


def body(
    start_values, cosine, arc_index, arc_weight, observed, orientation_term, step_gain, step_damp
):
    sizes = (lax.axis_size("row"), lax.axis_size("col"), start_values.shape[0], cosine.shape[0])
    split, lhs_hi, lhs_lo, rhs = gather(
        sizes,
        arc_weight,
        start_values,
        cosine.reshape(1, -1),
        arc_index.reshape(1, -1),
        observed.reshape(1, -1),
        step_gain,
        step_damp,
        orientation_term,
    )
    return multiply(sizes, lhs_hi, lhs_lo, split), rhs.reshape(sizes[2], 1, LANES)


def solution(mesh):
    in_specs = (
        P(None, "col", None, "row"),
        P("row"),
        P("row"),
        P(),
        P("row"),
        P("row", None, "col", None),
        P(),
        P(),
    )
    out_specs = (P(None, "row", None, "col"), P(None, "col", None))
    return jax.shard_map(body, mesh=mesh, in_specs=in_specs, out_specs=out_specs, check_vma=False)
```

profile of v0, /device:TPU:9, one launch (start us, length us, event | category | flops | bytes accessed | tf_op | source)
XLA Modules:
  0.0 100.5 jit_solution(1888757447830167757)
XLA Ops:
  0.6 1.5 %copy.10.start = f32[44,1,2,32]{3,2,1,0:T(2,128)} copy(f32[44,1,2,32]{0,3,2,1:T(8,128)} %param.8) | data formatting | bytes 22528 | tf_op args[0]
  2.1 68.4 %gather_design.1 = (bf16[44,512,128]{2,1,0:T(8,128)(2,1)}, bf16[512,512]{1,0:T(8,128)(2,1)}, bf16[512,256]{1,0:T(8,128)(2,1)}, f32[44,128]{1,0:T(8,128)}) custom-call(f32[8]{0:T(128)} %arc_weight.1, f32[44,1,2,32]{3,2,1,0:T(2,128)} %copy.10.start, f32[1,32]{1,0:T(1,128)} %bitcast.5, s32[1,32]{1,0:T(1,128)} %bitcast.6, f32[1,32]{1,0:T(1,128)} %bitcast.7, ...), custom_call_target="tpu_custom_call" | custom-call | tf_op jit(solution)/shard_map/gather_design/pallas_call | solution.py:326
  70.5 1.4 %copy.12 = f32[44,1,128]{2,1,0:T(1,128)} copy(f32[44,1,128]{2,0,1:T(8,128)} %bitcast.4) | data formatting | bytes 45056
  71.9 0.0 copy-start
  71.9 1.0 %copy-done = bf16[512,512]{1,0:T(8,128)(2,1)S(1)} copy-done((bf16[512,512]{1,0:T(8,128)(2,1)S(1)}, bf16[512,512]{1,0:T(8,128)(2,1)}, u32[]{:S(2)}) %copy-start) | copy-done | bytes 524312
  72.9 0.0 copy-start.1
  72.9 0.9 copy-done.1
  73.9 14.1 %slab_product.1 = f32[4,128,44,128]{3,2,1,0:T(8,128)} custom-call(bf16[512,512]{1,0:T(8,128)(2,1)S(1)} %copy-done, bf16[512,256]{1,0:T(8,128)(2,1)S(1)} %copy-done.1, bf16[44,512,128]{2,1,0:T(8,128)(2,1)} %get-tuple-element.8.split), custom_call_target="tpu_custom_call" | custom-call | tf_op jit(solution)/shard_map/slab_product/pallas_call | solution.py:372
  88.0 12.5 %copy.11 = f32[4,128,44,128]{3,1,2,0:T(8,128)} copy(f32[4,128,44,128]{3,2,1,0:T(8,128)} %slab_product.1) | data formatting | bytes 23068672
Async XLA Ops:
  71.9 1.0 %copy-start = (bf16[512,512]{1,0:T(8,128)(2,1)S(1)}, bf16[512,512]{1,0:T(8,128)(2,1)}, u32[]{:S(2)}) copy-start(bf16[512,512]{1,0:T(8,128)(2,1)} %get-tuple-element.6.lhs_hi) | copy-start | bytes 1572868
  72.9 0.9 copy-start.1
where the time goes:
time: 101 us
  Pallas kernels  82.5 us (82%)
  local copies, waits for them, and re-layouts  17.4 us (17%)
    pallas_call x1, Pallas kernels, gather(): pl.pallas_call(functools.partial(gather_kernel, sizes), out_shape=(jax.Sh...  68.4 us
    unnamed x7, local copies, waits for them, and re-layouts  17.4 us
    pallas_call x1, Pallas kernels, multiply(): pl.pallas_call(functools.partial(multiply_kernel, total), grid=(pl.cdiv(t...  14.1 us

commit v1 on v0

--- a/solution.py
+++ b/solution.py
@@ -7,6 +7,8 @@
 from jax.sharding import PartitionSpec as P
 
 RT = 4
+FIRST = (2, 3)
+BATCH = 6
 LANES = 128
 MESH = pl.DeviceIdType.MESH
 
@@ -15,7 +17,7 @@
     sizes,
     arc_weight, start, cosine, arc_index, observed, gain, damp, orient,
     split_out, lhs_hi, lhs_lo, rhs_out,
-    every, split, forcing, f_t, g_t, d_t, q_t, slab, wsend, wblocks, wcol, ocol,
+    every, split, forcing, padded, starts, f_t, g_t, d_t, q_t, slab, wsend, wblocks, wcol, ocol,
     fsem, osem, rsem, xsem, wrsem, slsem, up_sem, down_sem, y_sem, x_send, w_send, sl_send,
 ):
     rows, cols, tiles, obs = sizes
@@ -99,27 +101,35 @@
         parts = [jnp.broadcast_to(ref[t * per + q, pl.ds(c, 1), :], (obs, LANES)) for q in range(per)]
         return jnp.concatenate(parts, axis=0).T
 
-    def recurrence(t):
-        for q in range(per):
-            fetch(t * per + q).wait()
-        f_t[...] = forcing[pl.ds(t * per, per)].reshape(LANES, LANES).T
-        g_t[...] = columns(gain, t) * cos_row
-        d_t[...] = columns(damp, t)
-        first = jnp.concatenate([start[t * per + q, 0, 0:1, :] for q in range(per)], axis=1)
-        second = jnp.concatenate([start[t * per + q, 0, 1:2, :] for q in range(per)], axis=1)
+    def recurrences(t0, count):
+        state = []
+        for k in range(count):
+            t = t0 + k
+            for q in range(per):
+                fetch(t * per + q).wait()
+            f_t[k] = forcing[pl.ds(t * per, per)].reshape(LANES, LANES).T
+            g_t[k] = columns(gain, t) * cos_row
+            d_t[k] = columns(damp, t)
+            for which in range(2):
+                rows_of = [starts[which, pl.ds(t * per + q, 1), :] for q in range(per)]
+                state.append(jnp.concatenate(rows_of, axis=1))
 
         def step(m, state):
-            prev_two, prev_one = state
-            for k in range(8):
-                at = pl.ds(m * 8 + k, 1)
-                current = g_t[at, :] * prev_one + (f_t[at, :] - d_t[at, :] * prev_two)
-                q_t[at, :] = current
-                prev_two, prev_one = prev_one, current
-            return prev_two, prev_one
-
-        lax.fori_loop(0, LANES // 8, step, (first, second))
+            state = list(state)
+            for i in range(8):
+                at = pl.ds(m * 8 + i, 1)
+                for k in range(count):
+                    prev_two, prev_one = state[2 * k], state[2 * k + 1]
+                    current = g_t[k, at, :] * prev_one + (f_t[k, at, :] - d_t[k, at, :] * prev_two)
+                    q_t[k, at, :] = current
+                    state[2 * k], state[2 * k + 1] = prev_one, current
+            return tuple(state)
+
+        lax.fori_loop(0, LANES // 8, step, tuple(state))
         own = pl.ds(pl.multiple_of(r * obs, obs), obs)
-        every[pl.ds(t * per, per), own, :] = q_t[...].T.reshape(per, obs, LANES)
+        for k in range(count):
+            t = t0 + k
+            every[pl.ds(t * per, per), own, :] = q_t[k].T.reshape(per, obs, LANES)
 
     def own_sends(t):
         @pl.when(u < line - 1)
@@ -133,7 +143,13 @@
         send(t, r, row_of(u, 1 - v), y_sem.at[0], rsem.at[r, t])
         relay(t, r)
 
-    recurrence(0)
+    for which in range(2):
+        padded[...] = jnp.zeros_like(padded)
+        padded[:, 0:tiles] = start[0, which]
+        starts[which] = padded[...].T
+
+    begun = FIRST[0]
+    recurrences(0, begun)
     pl.semaphore_wait(barrier, rows - 1 + cols - 1)
     for d in range(1, rows):
         pltpu.make_async_remote_copy(
@@ -145,12 +161,17 @@
             device_id_type=MESH,
         ).start()
     wblocks[r] = wsend[...]
-    own_sends(0)
-
-    @pl.loop(1, chunks)
-    def _(t):
-        recurrence(t)
+    for t in range(begun):
         own_sends(t)
+    while begun < chunks:
+        count = min(chunks - begun, FIRST[1] if begun == FIRST[0] else BATCH)
+        recurrences(begun, count)
+
+        @pl.loop(begun, begun + count)
+        def _(t):
+            own_sends(t)
+
+        begun += count
 
     for p in range(1, line):
         @pl.loop(0, chunks)
@@ -250,7 +271,7 @@
         def _(q):
             j = t * per + q
             values = every[j]
-            rhs_out[pl.ds(j, 1), :] = jnp.sum(values * ocol[...], axis=0, keepdims=True)
+            rhs_out[j] = jnp.sum(values * ocol[...], axis=0, keepdims=True)
             high = values.astype(jnp.bfloat16)
             split[j, 0:total, :] = high
             split[j, total:2 * total, :] = (values - high.astype(jnp.float32)).astype(jnp.bfloat16)
@@ -322,14 +343,14 @@
     anywhere = pl.BlockSpec(memory_space=pl.ANY)
     smem = pl.BlockSpec(memory_space=pltpu.SMEM)
     dma = pltpu.SemaphoreType.DMA
-    square = pltpu.VMEM((LANES, LANES), jnp.float32)
+    squares = pltpu.VMEM((BATCH, LANES, LANES), jnp.float32)
     return pl.pallas_call(
         functools.partial(gather_kernel, sizes),
         out_shape=(
             jax.ShapeDtypeStruct((tiles, 2 * total, LANES), jnp.bfloat16),
             jax.ShapeDtypeStruct((RT * LANES, 2 * total), jnp.bfloat16),
             jax.ShapeDtypeStruct((RT * LANES, total), jnp.bfloat16),
-            jax.ShapeDtypeStruct((tiles, LANES), jnp.float32),
+            jax.ShapeDtypeStruct((tiles, 1, LANES), jnp.float32),
         ),
         in_specs=[smem] + [vmem] * 6 + [anywhere],
         out_specs=(anywhere, vmem, vmem, vmem),
@@ -337,7 +358,9 @@
             pltpu.VMEM((tiles, total, LANES), jnp.float32),
             pltpu.VMEM((tiles, 2 * total, LANES), jnp.bfloat16),
             pltpu.VMEM((tiles, obs, LANES), jnp.float32),
-            square, square, square, square,
+            pltpu.VMEM((obs, LANES), jnp.float32),
+            pltpu.VMEM((2, LANES, obs), jnp.float32),
+            squares, squares, squares, squares,
             pltpu.VMEM((RT, total, LANES), jnp.float32),
             pltpu.VMEM((8, LANES), jnp.float32),
             pltpu.VMEM((rows, 8, LANES), jnp.float32),
@@ -354,34 +377,41 @@
     )(*operands)
 
 
-def multiply_kernel(total, lhs_hi, lhs_lo, split, out):
-    count = split.shape[0]
-    for j in range(0, count, 2):
+def multiply_kernel(total, lhs_hi, lhs_lo, split, rhs, out, rhs_out):
+    rhs_out[...] = rhs[...]
+    for j in range(0, split.shape[0], 2):
         pair = jnp.concatenate([split[j], split[j + 1]], axis=1)
         product = jnp.dot(lhs_hi[...], pair, preferred_element_type=jnp.float32)
         product += jnp.dot(lhs_lo[...], pair[0:total], preferred_element_type=jnp.float32)
         for k in range(2):
             piece = product[:, k * LANES:(k + 1) * LANES]
-            out[:, :, j + k, :] = piece.reshape(RT, LANES, LANES)
-
-
-def multiply(sizes, lhs_hi, lhs_lo, split):
+            out[:, j + k] = piece.reshape(RT, LANES, LANES)
+
+
+def multiply(sizes, lhs_hi, lhs_lo, split, rhs):
     rows, cols, tiles, obs = sizes
     total = rows * obs
-    group = 8
+    group = 4
     return pl.pallas_call(
         functools.partial(multiply_kernel, total),
-        grid=(pl.cdiv(tiles, group),),
-        out_shape=jax.ShapeDtypeStruct((RT, LANES, tiles, LANES), jnp.float32),
+        grid=(tiles // group,),
+        out_shape=(
+            jax.ShapeDtypeStruct((RT, tiles, LANES, LANES), jnp.float32),
+            jax.ShapeDtypeStruct(rhs.shape, jnp.float32),
+        ),
         in_specs=[
             pl.BlockSpec(lhs_hi.shape, lambda g: (0, 0)),
             pl.BlockSpec(lhs_lo.shape, lambda g: (0, 0)),
             pl.BlockSpec((group, 2 * total, LANES), lambda g: (g, 0, 0)),
+            pl.BlockSpec((group, 1, LANES), lambda g: (g, 0, 0)),
         ],
-        out_specs=pl.BlockSpec((RT, LANES, group, LANES), lambda g: (0, 0, g, 0)),
-        compiler_params=pltpu.CompilerParams(vmem_limit_bytes=48 << 20),
+        out_specs=(
+            pl.BlockSpec((RT, group, LANES, LANES), lambda g: (0, g, 0, 0)),
+            pl.BlockSpec((group, 1, LANES), lambda g: (g, 0, 0)),
+        ),
+        compiler_params=pltpu.CompilerParams(vmem_limit_bytes=60 << 20),
         name="slab_product",
-    )(lhs_hi, lhs_lo, split)
+    )(lhs_hi, lhs_lo, split, rhs)
 
 
 def body(
@@ -391,7 +421,7 @@
     split, lhs_hi, lhs_lo, rhs = gather(
         sizes,
         arc_weight,
-        start_values,
+        jnp.transpose(start_values, (1, 2, 3, 0)),
         cosine.reshape(1, -1),
         arc_index.reshape(1, -1),
         observed.reshape(1, -1),
@@ -399,7 +429,8 @@
         step_damp,
         orientation_term,
     )
-    return multiply(sizes, lhs_hi, lhs_lo, split), rhs.reshape(sizes[2], 1, LANES)
+    normal, rhs = multiply(sizes, lhs_hi, lhs_lo, split, rhs)
+    return jnp.transpose(normal, (0, 2, 1, 3)), rhs
 
 
 def solution(mesh):

time: 101 us -> 82.5 us (0.82)
  local copies, waits for them, and re-layouts: 17.4 us -> 0 us
  Pallas kernels: 82.5 us -> 81.4 us
    unnamed x7 -> x0, local copies, waits for them, and re-layouts: 17.4 us -> none
    pallas_call x1, Pallas kernels: 14.1 us -> 13 us  [multiply(): pl.pallas_call(functools.partial(multiply_kernel, total), grid=(tiles //...]
where the time goes in v1:
time: 82.5 us; the launch traced here: 82.1 us
  Pallas kernels  81.4 us (99%)
    pallas_call x1, Pallas kernels, gather(): pl.pallas_call(functools.partial(gather_kernel, sizes), out_shape=(jax.Sh...  68.5 us
    pallas_call x1, Pallas kernels, multiply(): pl.pallas_call(functools.partial(multiply_kernel, total), grid=(tiles //...  13 us

profile of v1, /device:TPU:9, one launch (start us, length us, event | category | flops | bytes accessed | tf_op | source)
XLA Modules:
  0.0 82.1 jit_solution(6498048747422272691)
XLA Ops:
  0.6 68.5 %gather_design.1 = (bf16[44,512,128]{2,1,0:T(8,128)(2,1)}, bf16[512,512]{1,0:T(8,128)(2,1)}, bf16[512,256]{1,0:T(8,128)(2,1)}, f32[44,1,128]{2,1,0:T(1,128)}) custom-call(f32[8]{0:T(128)} %arc_weight.1, f32[1,2,32,44]{3,2,1,0:T(8,128)} %bitcast.5, f32[1,32]{1,0:T(1,128)} %bitcast.6, s32[1,32]{1,0:T(1,128)} %bitcast.7, f32[1,32]{1,0:T(1,128)} %bitcast.8, ...), custom_call_target="tpu_custom_call" | custom-call | tf_op jit(solution)/shard_map/gather_design/pallas_call | solution.py:347
  69.1 13.0 %slab_product.1 = (f32[4,44,128,128]{3,2,1,0:T(8,128)}, f32[44,1,128]{2,1,0:T(1,128)}) custom-call(bf16[512,512]{1,0:T(8,128)(2,1)} %get-tuple-element.8.lhs_hi, bf16[512,256]{1,0:T(8,128)(2,1)} %get-tuple-element.9.lhs_lo, bf16[44,512,128]{2,1,0:T(8,128)(2,1)} %get-tuple-element.10.split, f32[44,1,128]{2,1,0:T(1,128)} %get-tuple-element.11.rhs), custom_call_target="tpu_custom_call" | custom-call | tf_op jit(solution)/shard_map/slab_product/pallas_call | solution.py:395

commit v2 on v1

--- a/solution.py
+++ b/solution.py
@@ -15,10 +15,11 @@
 
 def gather_kernel(
     sizes,
-    arc_weight, start, cosine, arc_index, observed, gain, damp, orient,
-    split_out, lhs_hi, lhs_lo, rhs_out,
-    every, split, forcing, padded, starts, f_t, g_t, d_t, q_t, slab, wsend, wblocks, wcol, ocol,
-    fsem, osem, rsem, xsem, wrsem, slsem, up_sem, down_sem, y_sem, x_send, w_send, sl_send,
+    arc_weight_in, start_in, cosine_in, arc_index_in, observed_in, gain_in, damp_in, orient,
+    split, hi, rhs_out,
+    arc_weight, start, cosine, arc_index, observed, gain, damp,
+    every, forcing, padded, starts, f_t, g_t, d_t, q_t, slab, wsend, wblocks, wcol, ocol,
+    isem, fsem, rsem, xsem, wrsem, slsem, up_sem, down_sem, y_sem, x_send, w_send, sl_send,
 ):
     rows, cols, tiles, obs = sizes
     line = rows // 2
@@ -38,6 +39,11 @@
     def row_of(uu, vv):
         return uu * 2 + vv
 
+    inputs = (arc_weight_in, start_in, cosine_in, arc_index_in, observed_in, gain_in, damp_in)
+    held = (arc_weight, start, cosine, arc_index, observed, gain, damp)
+    loads = [pltpu.make_async_copy(a, b, isem.at[k]) for k, (a, b) in enumerate(zip(inputs, held))]
+    for copy in loads:
+        copy.start()
     barrier = pltpu.get_barrier_semaphore()
     for d in range(1, rows):
         pl.semaphore_signal(barrier, inc=1, device_id=((r + d) % rows, c), device_id_type=MESH)
@@ -51,10 +57,12 @@
     def _(j):
         fetch(j).start()
 
+    for copy in loads:
+        copy.wait()
     index = arc_index[...]
     weight = jnp.zeros(index.shape, jnp.float32)
-    for k in range(arc_weight.shape[0]):
-        weight = weight + jnp.where(index == k, arc_weight[k], 0.0)
+    for k in range(arc_weight.shape[1]):
+        weight = weight + jnp.where(index == k, arc_weight[:, k:k + 1], 0.0)
     wsend[...] = jnp.zeros_like(wsend)
     wsend[0:1, 0:obs] = weight
     wsend[1:2, 0:obs] = weight * observed[...]
@@ -241,9 +249,29 @@
 
     total = rows * obs
 
-    def put(t):
-        spot = pl.ds(t * per, per)
-        return pltpu.make_async_copy(split.at[spot], split_out.at[spot], osem.at[t])
+    def left_side():
+        @pl.when(c == owner)
+        def _():
+            @pl.loop(0, RT)
+            def _(i):
+                slab[i] = every[slab_tile(i)]
+
+        @pl.when(c != owner)
+        def _():
+            @pl.loop(0, rows)
+            def _(src):
+                @pl.loop(0, RT)
+                def _(i):
+                    ref = slab.at[i, pl.ds(pl.multiple_of(src * obs, obs), obs), :]
+                    pltpu.make_async_copy(ref, ref, slsem.at[i, src]).wait()
+
+        for i in range(RT):
+            turned = (slab[i] * wcol[...]).T
+            high = turned.astype(jnp.bfloat16)
+            at = slice(i * LANES, (i + 1) * LANES)
+            hi[at, 0:total] = high
+            hi[at, total:2 * total] = high
+            hi[at, 2 * total:3 * total] = (turned - high.astype(jnp.float32)).astype(jnp.bfloat16)
 
     @pl.loop(0, chunks)
     def _(t):
@@ -267,6 +295,8 @@
                         arrived(t, src, rsem.at[src, t])
                     relay(t, src)
 
+        pl.when(t == chunks - 1)(left_side)
+
         @pl.loop(0, per)
         def _(q):
             j = t * per + q
@@ -275,31 +305,6 @@
             high = values.astype(jnp.bfloat16)
             split[j, 0:total, :] = high
             split[j, total:2 * total, :] = (values - high.astype(jnp.float32)).astype(jnp.bfloat16)
-
-        put(t).start()
-
-    @pl.when(c == owner)
-    def _():
-        @pl.loop(0, RT)
-        def _(i):
-            slab[i] = every[slab_tile(i)]
-
-    @pl.when(c != owner)
-    def _():
-        @pl.loop(0, rows)
-        def _(src):
-            @pl.loop(0, RT)
-            def _(i):
-                ref = slab.at[i, pl.ds(pl.multiple_of(src * obs, obs), obs), :]
-                pltpu.make_async_copy(ref, ref, slsem.at[i, src]).wait()
-
-    for i in range(RT):
-        turned = (slab[i] * wcol[...]).T
-        high = turned.astype(jnp.bfloat16)
-        at = slice(i * LANES, (i + 1) * LANES)
-        lhs_hi[at, 0:total] = high
-        lhs_hi[at, total:2 * total] = high
-        lhs_lo[at, :] = (turned - high.astype(jnp.float32)).astype(jnp.bfloat16)
 
     def left(sem, low=0, count=tiles):
         ref = every.at[pl.ds(low, count), pl.ds(0, obs), :]
@@ -328,10 +333,6 @@
         for d in range(1, cols):
             pltpu.make_async_copy(slab, slab, sl_send.at[d]).wait()
 
-    @pl.loop(0, chunks)
-    def _(t):
-        put(t).wait()
-
 
 def gather(sizes, *operands):
     rows, cols, tiles, obs = sizes
@@ -340,23 +341,21 @@
     chunks = tiles // per
     line = rows // 2
     vmem = pl.BlockSpec(memory_space=pltpu.VMEM)
-    anywhere = pl.BlockSpec(memory_space=pl.ANY)
-    smem = pl.BlockSpec(memory_space=pltpu.SMEM)
+    held = [pltpu.VMEM(x.shape, x.dtype) for x in operands[:-1]]
     dma = pltpu.SemaphoreType.DMA
     squares = pltpu.VMEM((BATCH, LANES, LANES), jnp.float32)
     return pl.pallas_call(
         functools.partial(gather_kernel, sizes),
         out_shape=(
-            jax.ShapeDtypeStruct((tiles, 2 * total, LANES), jnp.bfloat16),
-            jax.ShapeDtypeStruct((RT * LANES, 2 * total), jnp.bfloat16),
-            jax.ShapeDtypeStruct((RT * LANES, total), jnp.bfloat16),
-            jax.ShapeDtypeStruct((tiles, 1, LANES), jnp.float32),
+            pltpu.VMEM((tiles, 2 * total, LANES), jnp.bfloat16),
+            pltpu.VMEM((RT * LANES, 3 * total), jnp.bfloat16),
+            pltpu.VMEM((tiles, 1, LANES), jnp.float32),
         ),
-        in_specs=[smem] + [vmem] * 6 + [anywhere],
-        out_specs=(anywhere, vmem, vmem, vmem),
+        in_specs=[pl.BlockSpec(memory_space=pltpu.HBM)] * len(operands),
+        out_specs=(vmem, vmem, vmem),
         scratch_shapes=[
+            *held,
             pltpu.VMEM((tiles, total, LANES), jnp.float32),
-            pltpu.VMEM((tiles, 2 * total, LANES), jnp.bfloat16),
             pltpu.VMEM((tiles, obs, LANES), jnp.float32),
             pltpu.VMEM((obs, LANES), jnp.float32),
             pltpu.VMEM((2, LANES, obs), jnp.float32),
@@ -366,61 +365,77 @@
             pltpu.VMEM((rows, 8, LANES), jnp.float32),
             pltpu.VMEM((total, LANES), jnp.float32),
             pltpu.VMEM((total, LANES), jnp.float32),
-            dma((tiles,)), dma((chunks,)), dma((rows, chunks)), dma((chunks,)), dma((rows,)),
+            dma((len(held),)), dma((tiles,)), dma((rows, chunks)), dma((chunks,)), dma((rows,)),
             dma((RT, rows)), dma((line,)), dma((line,)), dma((2 * line,)), dma(()), dma((rows,)),
             dma((cols,)),
         ],
         compiler_params=pltpu.CompilerParams(
-            collective_id=0, has_side_effects=True, vmem_limit_bytes=56 << 20
+            collective_id=0, has_side_effects=True, vmem_limit_bytes=32 << 20
         ),
         name="gather_design",
-    )(*operands)
-
-
-def multiply_kernel(total, lhs_hi, lhs_lo, split, rhs, out, rhs_out):
+    )(*(pltpu.with_memory_space_constraint(x, pltpu.HBM) for x in operands))
+
+
+def multiply_kernel(group, lhs, held, rhs, out, rhs_out, result, osem):
+    tiles, depth, _ = held.shape
+    total = depth // 2
+    steps = tiles // group
+
+    def store(t):
+        spot = pl.ds(t * group, group)
+        return pltpu.make_async_copy(result.at[:, spot], out.at[:, spot], osem.at[t])
+
+    @pl.loop(0, steps)
+    def _(t):
+        for k in range(0, group, 2):
+            j = t * group + k
+            pair = jnp.concatenate([held[j], held[j + 1]], axis=1)
+            depths = jnp.concatenate([pair, pair[0:total]], axis=0)
+            product = jnp.dot(lhs[...], depths, preferred_element_type=jnp.float32)
+            for n in range(2):
+                piece = product[:, n * LANES:(n + 1) * LANES]
+                result[:, j + n] = piece.reshape(RT, LANES, LANES)
+        store(t).start()
+
     rhs_out[...] = rhs[...]
-    for j in range(0, split.shape[0], 2):
-        pair = jnp.concatenate([split[j], split[j + 1]], axis=1)
-        product = jnp.dot(lhs_hi[...], pair, preferred_element_type=jnp.float32)
-        product += jnp.dot(lhs_lo[...], pair[0:total], preferred_element_type=jnp.float32)
-        for k in range(2):
-            piece = product[:, k * LANES:(k + 1) * LANES]
-            out[:, j + k] = piece.reshape(RT, LANES, LANES)
-
-
-def multiply(sizes, lhs_hi, lhs_lo, split, rhs):
-    rows, cols, tiles, obs = sizes
-    total = rows * obs
+
+    @pl.loop(0, steps)
+    def _(t):
+        store(t).wait()
+
+
+def multiply(sizes, lhs, split, rhs):
+    tiles = sizes[2]
     group = 4
+    steps = tiles // group
+    vmem = pl.BlockSpec(memory_space=pltpu.VMEM)
+    anywhere = pl.BlockSpec(memory_space=pl.ANY)
+    dma = pltpu.SemaphoreType.DMA
+    product_shape = (RT, tiles, LANES, LANES)
     return pl.pallas_call(
-        functools.partial(multiply_kernel, total),
-        grid=(tiles // group,),
+        functools.partial(multiply_kernel, group),
         out_shape=(
-            jax.ShapeDtypeStruct((RT, tiles, LANES, LANES), jnp.float32),
+            jax.ShapeDtypeStruct(product_shape, jnp.float32),
             jax.ShapeDtypeStruct(rhs.shape, jnp.float32),
         ),
-        in_specs=[
-            pl.BlockSpec(lhs_hi.shape, lambda g: (0, 0)),
-            pl.BlockSpec(lhs_lo.shape, lambda g: (0, 0)),
-            pl.BlockSpec((group, 2 * total, LANES), lambda g: (g, 0, 0)),
-            pl.BlockSpec((group, 1, LANES), lambda g: (g, 0, 0)),
+        in_specs=[vmem, vmem, vmem],
+        out_specs=(anywhere, vmem),
+        scratch_shapes=[
+            pltpu.VMEM(product_shape, jnp.float32),
+            dma((steps,)),
         ],
-        out_specs=(
-            pl.BlockSpec((RT, group, LANES, LANES), lambda g: (0, g, 0, 0)),
-            pl.BlockSpec((group, 1, LANES), lambda g: (g, 0, 0)),
-        ),
-        compiler_params=pltpu.CompilerParams(vmem_limit_bytes=60 << 20),
+        compiler_params=pltpu.CompilerParams(vmem_limit_bytes=32 << 20),
         name="slab_product",
-    )(lhs_hi, lhs_lo, split, rhs)
+    )(*(pltpu.with_memory_space_constraint(x, pltpu.VMEM) for x in (lhs, split, rhs)))
 
 
 def body(
     start_values, cosine, arc_index, arc_weight, observed, orientation_term, step_gain, step_damp
 ):
     sizes = (lax.axis_size("row"), lax.axis_size("col"), start_values.shape[0], cosine.shape[0])
-    split, lhs_hi, lhs_lo, rhs = gather(
+    split, lhs, rhs = gather(
         sizes,
-        arc_weight,
+        arc_weight.reshape(1, -1),
         jnp.transpose(start_values, (1, 2, 3, 0)),
         cosine.reshape(1, -1),
         arc_index.reshape(1, -1),
@@ -429,7 +444,7 @@
         step_damp,
         orientation_term,
     )
-    normal, rhs = multiply(sizes, lhs_hi, lhs_lo, split, rhs)
+    normal, rhs = multiply(sizes, lhs, split, rhs)
     return jnp.transpose(normal, (0, 2, 1, 3)), rhs
 
 

time: 82.5 us -> 75.4 us (0.914)
  Pallas kernels: 81.4 us -> 74.6 us
    pallas_call x2, Pallas kernels: 81.4 us -> 74.6 us  [the longest x1 66.6 us: gather(): pl.pallas_call(functools.partial(gather_kernel, sizes), out_shape=(pltpu....]
where the time goes in v2:
time: 75.4 us; the launch traced here: 75.3 us
  Pallas kernels  74.6 us (99%)
    pallas_call x1, Pallas kernels, gather(): pl.pallas_call(functools.partial(gather_kernel, sizes), out_shape=(pltpu....  66.6 us
    pallas_call x1, Pallas kernels, multiply(): pl.pallas_call(functools.partial(multiply_kernel, group), out_shape=(jax....  8.02 us

profile of v2, /device:TPU:9, one launch (start us, length us, event | category | flops | bytes accessed | tf_op | source)
XLA Modules:
  0.0 75.3 jit_solution(18122154010286728042)
XLA Ops:
  0.6 66.6 %gather_design.1 = (bf16[44,512,128]{2,1,0:T(8,128)(2,1)S(1)}, bf16[512,768]{1,0:T(8,128)(2,1)S(1)}, f32[44,1,128]{2,1,0:T(1,128)S(1)}) custom-call(f32[1,8]{1,0:T(1,128)} %bitcast.7, f32[1,2,32,44]{3,2,1,0:T(8,128)} %bitcast.6, f32[1,32]{1,0:T(1,128)} %bitcast.8, s32[1,32]{1,0:T(1,128)} %bitcast.9, f32[1,32]{1,0:T(1,128)} %bitcast.10, ...), custom_call_target="tpu_custom_call" | custom-call | tf_op jit(solution)/shard_map/gather_design/pallas_call | solution.py:347
  67.2 8.0 %slab_product.1 = (f32[4,44,128,128]{3,2,1,0:T(8,128)}, f32[44,1,128]{2,1,0:T(1,128)}) custom-call(bf16[512,768]{1,0:T(8,128)(2,1)S(1)} %get-tuple-element.7.lhs, bf16[44,512,128]{2,1,0:T(8,128)(2,1)S(1)} %get-tuple-element.8.held, f32[44,1,128]{2,1,0:T(1,128)S(1)} %get-tuple-element.9.rhs), custom_call_target="tpu_custom_call" | custom-call | tf_op jit(solution)/shard_map/slab_product/pallas_call | solution.py:415
